TPU v7x, 256 devices: a whole 4x4x8 slice. The times are simulated.
256 devices in a mesh: inst: 32 (over x, y, core), tp: 8 (over z).
Axes of the slice: x: 4, y: 4, z: 8, core: 2. Of those that a mesh axis runs over, the one named last changes fastest.
Arguments:
- queries: bfloat16 [32, 8192], P('inst', 'tp'), may hold values from -8 to 8
- cache_keys: bfloat16 [64, 8, 4096, 128], P('inst', 'tp'), may hold values from -8 to 8
- cache_values: bfloat16 [64, 8, 4096, 128], P('inst', 'tp'), may hold values from -6 to 6
- block_request: int32 [64], replicated, may hold values from 0 to 7, as said below
- block_fill: int32 [64], replicated, may hold values from 1 to 4096
- out_weight: bfloat16 [8192, 4096], P('tp'), may hold values from -0.25 to 0.25
Outputs:
- mixed: bfloat16 [32, 4096], P('inst', 'tp')
Inputs may be any that keep to these rules, and one draw needn't show every extreme that they name: `block_request`: every request 0 to 7 has at least one stored block.
All inputs are finite; a program needn't handle non-finite values.
Results may differ from a plain program's by a relative error of at most 0.0075.
Values may be sent and summed in bfloat16 or wider, within the bound.
A program may use at most 64 MiB of HBM per device.

v0:
```python
import jax
import jax.numpy as jnp
from jax import lax
from jax.sharding import PartitionSpec as P

HQ = 64
KVH = 8
STEPS = 4


NEGATIVE_FILL = -1e30


def slot_partials(chosen_rows, key_slots, value_slots, fill_counts):
    slot_count = key_slots.shape[0]
    kv_local = key_slots.shape[1]
    block_len = key_slots.shape[2]
    head_size = key_slots.shape[3]
    group_size = HQ // KVH
    query_block = chosen_rows.reshape(slot_count, STEPS, kv_local, group_size, head_size)
    query_block = query_block.transpose(0, 2, 1, 3, 4).reshape(
        slot_count, kv_local, STEPS * group_size, head_size
    )
    scores = jnp.einsum(
        "bkqd,bktd->bkqt", query_block, key_slots, preferred_element_type=jnp.float32
    ) * head_size ** (-0.5)
    valid_mask = jnp.arange(block_len, dtype=jnp.int32)[None, :] < fill_counts[:, None]
    scores = jnp.where(valid_mask[:, None, None, :], scores, NEGATIVE_FILL)
    maxima = jnp.max(scores, axis=-1)
    probabilities = jnp.exp(scores - maxima[..., None]).astype(jnp.bfloat16)
    totals = jnp.sum(probabilities.astype(jnp.float32), axis=-1)
    outputs = jnp.einsum(
        "bkqt,bktd->bkqd", probabilities, value_slots, preferred_element_type=jnp.float32
    )
    local_heads = kv_local * group_size
    maxima = (
        maxima.reshape(slot_count, kv_local, STEPS, group_size)
        .transpose(0, 2, 1, 3)
        .reshape(slot_count, STEPS, local_heads)
    )
    totals = (
        totals.reshape(slot_count, kv_local, STEPS, group_size)
        .transpose(0, 2, 1, 3)
        .reshape(slot_count, STEPS, local_heads)
    )
    outputs = outputs.reshape(slot_count, kv_local, STEPS, group_size, head_size).transpose(
        0, 2, 1, 3, 4
    )
    return (maxima, totals, outputs.reshape(slot_count, STEPS, local_heads, head_size))


def body(queries, cache_keys, cache_values, block_request, block_fill, out_weight):
    lender = lax.axis_index("inst")
    places = lax.axis_size("inst")
    request_count = places // STEPS
    slot_count = cache_keys.shape[0]
    held_blocks = lax.dynamic_slice_in_dim(block_request, lender * slot_count, slot_count)
    fill_counts = lax.dynamic_slice_in_dim(block_fill, lender * slot_count, slot_count)
    every_query = lax.all_gather(queries, "inst", axis=0, tiled=True)
    query_table = every_query.reshape(request_count, STEPS, every_query.shape[1])
    chosen_rows = jnp.take(query_table, held_blocks, axis=0)
    maxima, totals, outputs = slot_partials(chosen_rows, cache_keys, cache_values, fill_counts)
    local_heads = maxima.shape[2]
    head_size = outputs.shape[3]
    my_request = lender // STEPS
    my_position = lender % STEPS
    run_top = jnp.full((local_heads,), NEGATIVE_FILL, jnp.float32)
    piece_top = lax.dynamic_index_in_dim(
        lax.all_gather(maxima, "inst", axis=0, tiled=True), my_position, 1, keepdims=False
    )
    piece_total = lax.dynamic_index_in_dim(
        lax.all_gather(totals, "inst", axis=0, tiled=True), my_position, 1, keepdims=False
    )
    piece_out = lax.dynamic_index_in_dim(
        lax.all_gather(outputs, "inst", axis=0, tiled=True), my_position, 1, keepdims=False
    )
    matches = (block_request == my_request)[:, None]
    new_top = jnp.maximum(run_top, jnp.max(jnp.where(matches, piece_top, NEGATIVE_FILL), axis=0))
    weights = jnp.where(matches, jnp.exp(jnp.minimum(piece_top - new_top, 0.0)), 0.0)
    new_total = jnp.sum(weights * piece_total, axis=0)
    new_out = jnp.sum(weights[..., None] * piece_out, axis=0)
    attention = (
        (new_out / new_total[..., None]).reshape(1, local_heads * head_size).astype(jnp.bfloat16)
    )
    projected = jnp.dot(attention, out_weight, preferred_element_type=jnp.float32)
    mixed = lax.psum_scatter(projected, "tp", scatter_dimension=1, tiled=True)
    return mixed.astype(jnp.bfloat16)


def solution(mesh):
    in_specs = (
        P("inst", "tp"),
        P("inst", "tp", None, None),
        P("inst", "tp", None, None),
        P(),
        P(),
        P("tp", None),
    )
    out_specs = P("inst", "tp")
    return jax.shard_map(body, mesh=mesh, in_specs=in_specs, out_specs=out_specs, check_vma=False)
```

profile of v0, /device:TPU:14, one launch (start us, length us, event | category | flops | bytes accessed | tf_op | source)
XLA Modules:
  0.0 145.0 jit_solution(9914999969771463775)
XLA Ops:
  6.5 0.0 copy-start
  6.5 0.0 all-gather.3.cloned.1.call-start
  6.5 0.9 dynamic_slice.17
  7.4 0.7 compare_and_fusion
  8.2 0.1 iota_compare_fusion
  8.3 22.6 %all-gather = bf16[32,1,1024]{2,1,0:T(2,128)(2,1)S(1)} all-gather(bf16[1,1,1024]{2,1,0:T(2,128)(2,1)} %bitcast.31), channel_id=1, replica_groups=mesh['inst'=32,'tp'=8] {'inst'}, dimensions={0}, use_global_device_ids=true | all-gather | bytes 67584 | tf_op jit(solution)/shard_map/all_gather | solution.py:59
  30.8 0.4 reduce.4
  31.2 0.6 gather_fusion
  31.8 0.0 copy-start.1
  31.8 0.0 copy-done
  31.8 1.0 fusion.13
  32.8 0.6 copy-done.1
  33.4 0.0 copy-start.2
  33.4 1.1 fusion.4
  34.5 0.0 all-gather.3.cloned.1.call-update
  34.6 0.0 reduce-scatter.4.cloned.1.call-start
  34.6 0.1 reshape_transpose_reshape.10
  34.7 0.3 convert_reduce_fusion
  35.0 0.1 reshape_transpose_reshape.12
  35.1 23.9 %all_gather.15 = f32[64,4,8]{2,1,0:T(4,128)S(1)} all-gather(f32[2,4,8]{2,1,0:T(4,128)S(1)} %reshape_transpose_reshape.12), channel_id=1, replica_groups=mesh['inst'=32,'tp'=8] {'inst'}, dimensions={0}, use_global_device_ids=true | all-gather | bytes 8448 | tf_op jit(solution)/shard_map/all_gather | solution.py:72
  59.0 22.3 %all_gather.13 = f32[64,4,8]{2,1,0:T(4,128)S(1)} all-gather(f32[2,4,8]{2,1,0:T(4,128)S(1)} %reshape_transpose_reshape.10), channel_id=1, replica_groups=mesh['inst'=32,'tp'=8] {'inst'}, dimensions={0}, use_global_device_ids=true | all-gather | bytes 8448 | tf_op jit(solution)/shard_map/all_gather | solution.py:69
  81.5 0.0 copy-done.2
  81.5 0.1 select_reduce_fusion
  81.6 0.1 multiply_reduce_fusion
  81.7 2.1 %all-gather.3.cloned.1.call-done = f32[64,4,8,128]{3,2,1,0:T(8,128)} async-done(((f32[2,4,8,128]{3,2,1,0:T(8,128)}), f32[64,4,8,128]{3,2,1,0:T(8,128)}) %all-gather.3.cloned.1.call-update) | async-done | bytes 1048592 | tf_op jit(solution)/shard_map/all_gather | solution.py:75
  83.8 1.1 fusion.7
  84.8 0.1 fusion.11
  84.9 8.1 %convolution_bitcast_fusion = f32[4096,1]{1,0:T(8,128)} fusion(bf16[1024,1]{0,1:T(2,128)(2,1)S(1)} %reshape.122, bf16[1024,4096]{1,0:T(8,128)(2,1)} %param.11), kind=kOutput, calls=%fused_computation.1 | convolution fusion | flops 8388608 | bytes 8407040
  93.0 0.0 reduce-scatter.4.cloned.1.call-update
  93.1 43.4 %reduce-scatter.4.cloned.1.call-done = f32[512,1]{1,0:T(8,128)} async-done(((f32[4096,1]{1,0:T(8,128)}), f32[512,1]{1,0:T(8,128)}) %reduce-scatter.4.cloned.1.call-update) | async-done | bytes 2064
  136.5 1.6 %copy.8 = bf16[1,512]{1,0:T(2,128)(2,1)} copy(f32[1,512]{0,1:T(8,128)} %bitcast.29) | data formatting | bytes 3072
  (8 shorter events, 0.1 us)
Async XLA Ops:
  6.5 25.3 %copy-start = (bf16[2,1,4096,128]{3,2,1,0:T(8,128)(2,1)S(1)}, bf16[2,1,4096,128]{3,2,1,0:T(8,128)(2,1)}, u32[]{:S(2)}) copy-start(bf16[2,1,4096,128]{3,2,1,0:T(8,128)(2,1)} %param.7) | copy-start | bytes 6291460
  6.5 77.2 %all-gather.3.cloned.1.call-start = ((), (), s32[]{:S(2)}) async-start(), calls=%async_computation.1 | async-start | bytes 1081344 | tf_op jit(solution)/shard_map/all_gather | solution.py:75
  31.8 1.6 %copy-start.1 = (bf16[2,1,4096,128]{3,2,1,0:T(8,128)(2,1)S(1)}, bf16[2,1,4096,128]{3,2,1,0:T(8,128)(2,1)}, u32[]{:S(2)}) copy-start(bf16[2,1,4096,128]{3,2,1,0:T(8,128)(2,1)} %param.8) | copy-start | bytes 6291460
  33.4 48.1 %copy-start.2 = (s32[64]{0:T(128)S(1)}, s32[64]{0:T(128)}, u32[]{:S(2)}) copy-start(s32[64]{0:T(128)} %param.9) | copy-start | bytes 772
  34.6 101.9 %reduce-scatter.4.cloned.1.call-start = ((), (), s32[]{:S(2)}) async-start(), calls=%async_computation.2 | async-start | bytes 2359296
Sparse Core Ops, SparseCore 0:
  34.7 49.0 all-gather.2
  93.2 43.2 reduce-scatter.3
where the time goes:
time: 145 us
  blocking collectives  68.8 us (47%)
  waiting for transfers between devices  45.5 us (31%)
  between operations  13.5 us (9%)
  matrix products  10.2 us (7%)
  local copies, waits for them, and re-layouts  4.02 us (3%)
  other arithmetic  2.85 us (2%)
    unnamed x3, waiting for transfers between devices  43.4 us
    all_gather x1, blocking collectives, body(): lax.all_gather(totals, 'inst', axis=0, tiled=True)  23.9 us
    all_gather x1, blocking collectives, body(): every_query = lax.all_gather(queries, 'inst', axis=0, tiled=True)  22.6 us
    all_gather x1, blocking collectives, body(): lax.all_gather(maxima, 'inst', axis=0, tiled=True)  22.3 us
    unnamed x1, matrix products  8.11 us
  transfers between devices with their start and end apart: 2, of which 2 were waited for; matrix products, arithmetic and copies ran while one was open for 1% of the time, Pallas kernels for 0%

commit v1 on v0

v1 whole, which is shorter than its diff:
```python
import math

import jax
import jax.numpy as jnp
from jax import lax
from jax.experimental import pallas as pl
from jax.experimental.pallas import tpu as pltpu
from jax.sharding import PartitionSpec as P

MESH = pl.DeviceIdType.MESH
EMPTY = -1e30


def kernel(
    n_inst,
    n_tp,
    req_ref,
    fill_ref,
    q_ref,
    k_hbm,
    v_hbm,
    w_hbm,
    out_ref,
    kbuf,
    vbuf,
    wbuf,
    q_all,
    msg,
    got,
    part,
    parts,
    local_sem,
    q_send,
    q_recv,
    m_send,
    m_recv,
    p_send,
    p_recv,
):
    me = lax.axis_index("inst")
    my_tp = lax.axis_index("tp")
    blocks, block_len, head_size = kbuf.shape
    heads = q_all.shape[1]
    steps = 4
    rows = steps * heads
    requests = n_inst // steps
    out_cols = out_ref.shape[1]
    scale = head_size**-0.5 * math.log2(math.e)

    k_copies = [
        pltpu.make_async_copy(k_hbm.at[b, 0], kbuf.at[b], local_sem.at[b]) for b in range(blocks)
    ]
    v_copies = [
        pltpu.make_async_copy(v_hbm.at[b, 0], vbuf.at[b], local_sem.at[blocks + b])
        for b in range(blocks)
    ]
    w_copy = pltpu.make_async_copy(w_hbm, wbuf, local_sem.at[2 * blocks])
    for c in k_copies + v_copies + [w_copy]:
        c.start()

    barrier = pltpu.get_barrier_semaphore()

    def greet_inst(i, _):
        pl.semaphore_signal(
            barrier, inc=1, device_id={"inst": lax.rem(me + i, n_inst)}, device_id_type=MESH
        )
        return 0

    def greet_tp(i, _):
        pl.semaphore_signal(
            barrier, inc=1, device_id={"tp": lax.rem(my_tp + i, n_tp)}, device_id_type=MESH
        )
        return 0

    lax.fori_loop(1, n_inst, greet_inst, 0)
    lax.fori_loop(1, n_tp, greet_tp, 0)

    for h in range(heads):
        q_all[me, h : h + 1, :] = q_ref[:, h * head_size : (h + 1) * head_size].astype(jnp.float32)

    pl.semaphore_wait(barrier, n_inst + n_tp - 2)

    def send_q(i, _):
        pltpu.make_async_remote_copy(
            src_ref=q_all.at[me],
            dst_ref=q_all.at[me],
            send_sem=q_send,
            recv_sem=q_recv,
            device_id={"inst": lax.rem(me + i, n_inst)},
            device_id_type=MESH,
        ).start()
        return 0

    lax.fori_loop(1, n_inst, send_q, 0)
    others = q_all.at[pl.ds(0, n_inst - 1)]
    pltpu.make_async_copy(others, others, q_recv).wait()
    pltpu.make_async_copy(others, others, q_send).wait()

    tops, totals, outs, owners = [], [], [], []
    for b in range(blocks):
        request = req_ref[me * blocks + b]
        fill = fill_ref[me * blocks + b]
        q = q_all[pl.ds(request * steps, steps)].reshape(rows, head_size).astype(jnp.bfloat16)
        k_copies[b].wait()
        s = lax.dot_general(
            q, kbuf[b], (((1,), (1,)), ((), ())), preferred_element_type=jnp.float32
        )
        used = lax.broadcasted_iota(jnp.int32, s.shape, 1) < fill
        s = jnp.where(used, s * scale, EMPTY)
        top = jnp.max(s, axis=1, keepdims=True).astype(jnp.bfloat16).astype(jnp.float32)
        p = jnp.exp2(s - top)
        total = jnp.sum(p, axis=1, keepdims=True)
        v_copies[b].wait()
        o = jnp.dot(p.astype(jnp.bfloat16), vbuf[b], preferred_element_type=jnp.float32)
        tops.append(top)
        totals.append(total)
        outs.append(o)
        owners.append(request)

    lane = lax.broadcasted_iota(jnp.int32, (rows, head_size), 1)

    def pack(top, total, o):
        o = o / total
        high = total.astype(jnp.bfloat16).astype(jnp.float32)
        stats = jnp.where(lane == 0, top, jnp.where(lane == 1, high, total - high))
        o = o.reshape(steps, heads, head_size)
        stats = stats.reshape(steps, heads, head_size)
        return jnp.concatenate([o, stats], axis=1)

    both_top = jnp.maximum(tops[0], tops[1])
    w0 = jnp.exp2(tops[0] - both_top)
    w1 = jnp.exp2(tops[1] - both_top)
    both = pack(both_top, w0 * totals[0] + w1 * totals[1], w0 * outs[0] + w1 * outs[1])
    same = owners[0] == owners[1]
    first = jnp.where(same, both, pack(tops[0], totals[0], outs[0]))
    second = jnp.where(same, both, pack(tops[1], totals[1], outs[1]))
    row = lax.broadcasted_iota(jnp.int32, first.shape, 1)
    lanes = lax.broadcasted_iota(jnp.int32, first.shape, 2)
    empty = jnp.where((row >= heads) & (lanes == 0), EMPTY, 0.0)
    for r in range(requests):
        tile = jnp.where(owners[0] == r, first, jnp.where(owners[1] == r, second, empty))
        msg[r * steps : (r + 1) * steps] = tile.astype(jnp.bfloat16)
    got[me] = msg[me]

    def send_m(i, _):
        peer = lax.rem(me + i, n_inst)
        pltpu.make_async_remote_copy(
            src_ref=msg.at[peer],
            dst_ref=got.at[me],
            send_sem=m_send,
            recv_sem=m_recv,
            device_id={"inst": peer},
            device_id_type=MESH,
        ).start()
        return 0

    lax.fori_loop(1, n_inst, send_m, 0)
    others = got.at[pl.ds(0, n_inst - 1)]
    pltpu.make_async_copy(others, others, m_recv).wait()
    pltpu.make_async_copy(others, others, m_send).wait()

    tile = got[...].astype(jnp.float32)
    o = tile[:, :heads]
    top = tile[:, heads:, 0:1]
    total = tile[:, heads:, 1:2] + tile[:, heads:, 2:3]
    best = jnp.max(top, axis=0, keepdims=True)
    weight = jnp.exp2(top - best) * total
    att = jnp.sum(weight * o, axis=0) / jnp.sum(weight, axis=0)
    att = jnp.concatenate([att[h : h + 1] for h in range(heads)], axis=1).astype(jnp.bfloat16)

    w_copy.wait()

    def project(i, _):
        peer = lax.rem(my_tp + i, n_tp)
        cols = pl.ds(pl.multiple_of(peer * out_cols, out_cols), out_cols)
        part[peer] = jnp.dot(att, wbuf[:, cols], preferred_element_type=jnp.float32)
        pltpu.make_async_remote_copy(
            src_ref=part.at[peer],
            dst_ref=parts.at[my_tp],
            send_sem=p_send,
            recv_sem=p_recv,
            device_id={"tp": peer},
            device_id_type=MESH,
        ).start()
        return 0

    lax.fori_loop(1, n_tp, project, 0)
    cols = pl.ds(pl.multiple_of(my_tp * out_cols, out_cols), out_cols)
    parts[my_tp] = jnp.dot(att, wbuf[:, cols], preferred_element_type=jnp.float32)
    others = parts.at[pl.ds(0, n_tp - 1)]
    pltpu.make_async_copy(others, others, p_recv).wait()
    pltpu.make_async_copy(others, others, p_send).wait()
    out_ref[...] = jnp.sum(parts[...], axis=0).astype(out_ref.dtype)


def solution(mesh):
    n_inst, n_tp = mesh.shape["inst"], mesh.shape["tp"]

    def body(queries, cache_keys, cache_values, block_request, block_fill, out_weight):
        blocks, _, block_len, head_size = cache_keys.shape
        width, dout = out_weight.shape
        heads = width // head_size
        cols = dout // n_tp
        any_spec = pl.BlockSpec(memory_space=pl.ANY)
        smem_spec = pl.BlockSpec(memory_space=pltpu.SMEM)
        vmem_spec = pl.BlockSpec(memory_space=pltpu.VMEM)
        dma = pltpu.SemaphoreType.DMA
        return pl.pallas_call(
            lambda *refs: kernel(n_inst, n_tp, *refs),
            out_shape=jax.ShapeDtypeStruct((1, cols), jnp.bfloat16),
            in_specs=[smem_spec, smem_spec, vmem_spec, any_spec, any_spec, any_spec],
            out_specs=vmem_spec,
            scratch_shapes=[
                pltpu.VMEM((blocks, block_len, head_size), jnp.bfloat16),
                pltpu.VMEM((blocks, block_len, head_size), jnp.bfloat16),
                pltpu.VMEM((width, dout), jnp.bfloat16),
                pltpu.VMEM((n_inst, heads, head_size), jnp.float32),
                pltpu.VMEM((n_inst, 2 * heads, head_size), jnp.bfloat16),
                pltpu.VMEM((n_inst, 2 * heads, head_size), jnp.bfloat16),
                pltpu.VMEM((n_tp, 1, cols), jnp.float32),
                pltpu.VMEM((n_tp, 1, cols), jnp.float32),
                dma((2 * blocks + 1,)),
                dma,
                dma,
                dma,
                dma,
                dma,
                dma,
            ],
            compiler_params=pltpu.CompilerParams(
                collective_id=0, has_side_effects=True, vmem_limit_bytes=60 * 1024 * 1024
            ),
            name="paged_decode",
        )(block_request, block_fill, queries, cache_keys, cache_values, out_weight)

    in_specs = (
        P("inst", "tp"),
        P("inst", "tp", None, None),
        P("inst", "tp", None, None),
        P(),
        P(),
        P("tp", None),
    )
    return jax.shard_map(
        body, mesh=mesh, in_specs=in_specs, out_specs=P("inst", "tp"), check_vma=False
    )
```

time: 145 us -> 31.2 us (0.22)
  the two profiles are of different devices: /device:TPU:14 before, /device:TPU:1 now
where the time goes in v1:
time: 31.2 us; the launch traced here: 31.1 us
  Pallas kernels  29.8 us (96%)
  local copies, waits for them, and re-layouts  1.26 us (4%)
    pallas_call x1, Pallas kernels, body(): pl.pallas_call(lambda *refs: kernel(n_inst, n_tp, *refs), out_shape=jax.S...  29.8 us
    unnamed x1, local copies, waits for them, and re-layouts  1.26 us

profile of v1, /device:TPU:1, one launch (start us, length us, event | category | flops | bytes accessed | tf_op | source)
XLA Modules:
  0.0 31.1 jit_solution(8758343036440203749)
XLA Ops:
  0.0 29.8 %paged_decode.1 = bf16[1,512]{1,0:T(2,128)(2,1)} custom-call(s32[64]{0:T(128)} %refs_0_.1, s32[64]{0:T(128)} %refs_1_.1, bf16[1,1024]{1,0:T(2,128)(2,1)} %refs_2_.1, bf16[2,1,4096,128]{3,2,1,0:T(8,128)(2,1)} %refs_3_.1, bf16[2,1,4096,128]{3,2,1,0:T(8,128)(2,1)} %refs_4_.1, bf16[1024,4096]{1,0:T(8,128)(2,1)} %refs_5_.1), custom_call_target="tpu_custom_call" | custom-call | tf_op jit(solution)/shard_map/paged_decode/pallas_call | solution.py:208
  29.8 1.3 %copy.8 = bf16[1,512]{1,0:T(2,128)(2,1)} copy(bf16[1,512]{1,0:T(2,128)(2,1)} %paged_decode.1) | data formatting | bytes 2048

commit v2 on v1

v2 whole, which is shorter than its diff:
```python
import math

import jax
import jax.numpy as jnp
from jax import lax
from jax.experimental import pallas as pl
from jax.experimental.pallas import tpu as pltpu
from jax.sharding import PartitionSpec as P

MESH = pl.DeviceIdType.MESH
EMPTY = -1e30
STEPS = 4
SIDE = 4


def ring(d, n):
    return min(d, n - d)


PLANE = sorted(
    [(x, y, c) for x in range(SIDE) for y in range(SIDE) for c in range(2)][1:],
    key=lambda d: -(ring(d[0], SIDE) + ring(d[1], SIDE) + 0.5 * d[2]),
)


def kernel(
    n_tp,
    req_hbm,
    fill_hbm,
    q_hbm,
    k_hbm,
    v_hbm,
    w_hbm,
    out_hbm,
    req_ref,
    fill_ref,
    q_in,
    kbuf,
    kt,
    vbuf,
    wbuf,
    q_all,
    msg,
    got,
    part,
    local_sem,
    q_send,
    q_recv,
    m_send,
    m_recv,
    p_send,
    p_recv,
):
    me = lax.axis_index("inst")
    my_tp = lax.axis_index("tp")
    blocks, block_len, head_size = kbuf.shape
    n_inst, heads, _ = q_all.shape
    rows = STEPS * heads
    requests = n_inst // STEPS
    out_cols = part.shape[2]
    scale = head_size**-0.5 * math.log2(math.e)
    f32, bf16 = jnp.float32, jnp.bfloat16

    my_x, my_y, my_core = me // (2 * SIDE), (me // 2) % SIDE, me % 2
    plane = [
        (((my_x + x) % SIDE) * SIDE + (my_y + y) % SIDE) * 2 + (my_core + c) % 2
        for x, y, c in PLANE
    ]
    z_ring = [
        (my_tp + d) % n_tp for d in sorted(range(1, n_tp), key=lambda d: -ring(d, n_tp))
    ]

    barrier = pltpu.get_barrier_semaphore()
    for peer in plane:
        pl.semaphore_signal(barrier, inc=1, device_id={"inst": peer}, device_id_type=MESH)
    for peer in z_ring:
        pl.semaphore_signal(barrier, inc=1, device_id={"tp": peer}, device_id_type=MESH)

    q_copy = pltpu.make_async_copy(q_hbm, q_in, local_sem.at[0])
    req_copy = pltpu.make_async_copy(req_hbm, req_ref, local_sem.at[1])
    fill_copy = pltpu.make_async_copy(fill_hbm, fill_ref, local_sem.at[2])
    k_copy = pltpu.make_async_copy(k_hbm.at[:, 0], kbuf, local_sem.at[3])
    v_copies = [
        pltpu.make_async_copy(
            v_hbm.at[b, 0],
            vbuf.at[:, pl.ds(b * head_size, head_size)],
            local_sem.at[4 + b],
        )
        for b in range(blocks)
    ]
    w_copy = pltpu.make_async_copy(w_hbm, wbuf, local_sem.at[4 + blocks])
    for c in [q_copy, k_copy, req_copy, fill_copy] + v_copies + [w_copy]:
        c.start()
    q_copy.wait()
    for h in range(heads):
        q_all[me, h : h + 1, :] = q_in[:, h * head_size : (h + 1) * head_size].astype(f32)
    pl.semaphore_wait(barrier, len(plane) + len(z_ring))

    for peer in plane:
        pltpu.make_async_remote_copy(
            src_ref=q_all.at[me],
            dst_ref=q_all.at[me],
            send_sem=q_send,
            recv_sem=q_recv,
            device_id={"inst": peer},
            device_id_type=MESH,
        ).start()

    k_copy.wait()
    for b in range(blocks):
        kt[b * head_size : (b + 1) * head_size, :] = kbuf[b].T
    req_copy.wait()
    fill_copy.wait()
    for c in v_copies:
        c.wait()
    request = [req_ref[me * blocks + b] for b in range(blocks)]
    fill = [fill_ref[me * blocks + b] for b in range(blocks)]

    q_others = q_all.at[pl.ds(0, n_inst - 1)]
    pltpu.make_async_copy(q_others, q_others, q_recv).wait()

    q = [q_all[pl.ds(r * STEPS, STEPS)].reshape(rows, head_size).astype(bf16) for r in request]
    zero = jnp.zeros_like(q[0])
    q = jnp.concatenate(
        [jnp.concatenate([q[0], zero], axis=1), jnp.concatenate([zero, q[1]], axis=1)], axis=0
    )
    s = jnp.dot(q, kt[...], preferred_element_type=f32)
    slot = lax.broadcasted_iota(jnp.int32, (rows, block_len), 1)
    s = jnp.concatenate(
        [jnp.where(slot < fill[b], s[b * rows : (b + 1) * rows], EMPTY) for b in range(blocks)],
        axis=0,
    )
    top = (jnp.max(s, axis=1, keepdims=True) * scale).astype(bf16).astype(f32)
    p = jnp.exp2(s * scale - top)
    total = jnp.sum(p, axis=1, keepdims=True)
    o = jnp.dot(p.astype(bf16), vbuf[...], preferred_element_type=f32)
    tops = [top[:rows], top[rows:]]
    totals = [total[:rows], total[rows:]]
    outs = [o[:rows, :head_size], o[rows:, head_size:]]

    lane = lax.broadcasted_iota(jnp.int32, (rows, head_size), 1)

    def pack(top, total, o):
        o = o * (1.0 / total)
        high = total.astype(bf16).astype(f32)
        stats = jnp.where(lane == 0, top, jnp.where(lane == 1, high, total - high))
        o = o.reshape(STEPS, heads, head_size)
        stats = stats.reshape(STEPS, heads, head_size)
        return jnp.concatenate([o, stats], axis=1).astype(bf16)

    both_top = jnp.maximum(tops[0], tops[1])
    w0 = jnp.exp2(tops[0] - both_top)
    w1 = jnp.exp2(tops[1] - both_top)
    both = pack(both_top, w0 * totals[0] + w1 * totals[1], w0 * outs[0] + w1 * outs[1])
    same = request[0] == request[1]
    first = jnp.where(same, both, pack(tops[0], totals[0], outs[0]))
    second = jnp.where(same, both, pack(tops[1], totals[1], outs[1]))
    row = lax.broadcasted_iota(jnp.int32, (STEPS, 2 * heads, head_size), 1)
    lanes = lax.broadcasted_iota(jnp.int32, (STEPS, 2 * heads, head_size), 2)
    empty = jnp.where((row >= heads) & (lanes == 0), EMPTY, 0.0).astype(bf16)
    for r in range(requests):
        msg[r * STEPS : (r + 1) * STEPS] = jnp.where(
            request[0] == r, first, jnp.where(request[1] == r, second, empty)
        )
    for peer in plane:
        pltpu.make_async_remote_copy(
            src_ref=msg.at[peer],
            dst_ref=got.at[me],
            send_sem=m_send,
            recv_sem=m_recv,
            device_id={"inst": peer},
            device_id_type=MESH,
        ).start()
    got[me] = msg[me]
    w_copy.wait()
    m_others = got.at[pl.ds(0, n_inst - 1)]
    pltpu.make_async_copy(m_others, m_others, m_recv).wait()

    tile = got[...].astype(f32)
    o = tile[:, :heads]
    top = tile[:, heads:, 0:1]
    total = tile[:, heads:, 1:2] + tile[:, heads:, 2:3]
    best = jnp.max(top, axis=0, keepdims=True)
    weight = jnp.exp2(top - best) * total
    att = jnp.sum(weight * o, axis=0) / jnp.sum(weight, axis=0)
    att = jnp.concatenate([att[h : h + 1] for h in range(heads)], axis=1).astype(bf16)

    for peer in z_ring + [my_tp]:
        cols = pl.ds(pl.multiple_of(peer * out_cols, out_cols), out_cols)
        part[peer] = jnp.dot(att, wbuf[:, cols], preferred_element_type=f32)
        if peer is not my_tp:
            pltpu.make_async_remote_copy(
                src_ref=part.at[peer],
                dst_ref=out_hbm.at[my_tp],
                send_sem=p_send,
                recv_sem=p_recv,
                device_id={"tp": peer},
                device_id_type=MESH,
            ).start()
    own = pltpu.make_async_copy(part.at[my_tp], out_hbm.at[my_tp], local_sem.at[0])
    own.start()
    pltpu.make_async_copy(q_others, q_others, q_send).wait()
    pltpu.make_async_copy(m_others, m_others, m_send).wait()
    p_others = part.at[pl.ds(0, n_tp - 1)]
    pltpu.make_async_copy(p_others, p_others, p_send).wait()
    own.wait()
    p_others = out_hbm.at[pl.ds(0, n_tp - 1)]
    pltpu.make_async_copy(p_others, p_others, p_recv).wait()


def add_up(parts_ref, out_ref):
    out_ref[...] = jnp.sum(parts_ref[...], axis=0).astype(out_ref.dtype)


def solution(mesh):
    n_inst, n_tp = mesh.shape["inst"], mesh.shape["tp"]

    def body(queries, cache_keys, cache_values, block_request, block_fill, out_weight):
        blocks, _, block_len, head_size = cache_keys.shape
        width, dout = out_weight.shape
        heads = width // head_size
        cols = dout // n_tp
        any_spec = pl.BlockSpec(memory_space=pl.ANY)
        dma = pltpu.SemaphoreType.DMA
        bf16, f32 = jnp.bfloat16, jnp.float32
        parts = pl.pallas_call(
            lambda *refs: kernel(n_tp, *refs),
            out_shape=jax.ShapeDtypeStruct((n_tp, 1, cols), f32),
            in_specs=[any_spec] * 6,
            out_specs=any_spec,
            scratch_shapes=[
                pltpu.SMEM(block_request.shape, jnp.int32),
                pltpu.SMEM(block_fill.shape, jnp.int32),
                pltpu.VMEM(queries.shape, bf16),
                pltpu.VMEM((blocks, block_len, head_size), bf16),
                pltpu.VMEM((blocks * head_size, block_len), bf16),
                pltpu.VMEM((block_len, blocks * head_size), bf16),
                pltpu.VMEM((width, dout), bf16),
                pltpu.VMEM((n_inst, heads, head_size), f32),
                pltpu.VMEM((n_inst, 2 * heads, head_size), bf16),
                pltpu.VMEM((n_inst, 2 * heads, head_size), bf16),
                pltpu.VMEM((n_tp, 1, cols), f32),
                dma((5 + blocks,)),
                dma,
                dma,
                dma,
                dma,
                dma,
                dma,
            ],
            compiler_params=pltpu.CompilerParams(
                collective_id=0, has_side_effects=True, vmem_limit_bytes=60 * 1024 * 1024
            ),
            name="paged_decode",
        )(block_request, block_fill, queries, cache_keys, cache_values, out_weight)
        return pl.pallas_call(
            add_up,
            out_shape=jax.ShapeDtypeStruct((1, cols), bf16),
            name="add_up",
        )(parts)

    in_specs = (
        P("inst", "tp"),
        P("inst", "tp", None, None),
        P("inst", "tp", None, None),
        P(),
        P(),
        P("tp", None),
    )
    return jax.shard_map(
        body, mesh=mesh, in_specs=in_specs, out_specs=P("inst", "tp"), check_vma=False
    )
```

time: 31.2 us -> 28.2 us (0.904)
  Pallas kernels: 29.8 us -> 28 us
  local copies, waits for them, and re-layouts: 1.26 us -> 0 us
    pallas_call x1 -> x2, Pallas kernels: 29.8 us -> 28 us  [the longest x1 26.7 us: body(): pl.pallas_call(lambda *refs: kernel(n_tp, *refs), out_shape=jax.ShapeDtyp...]
    unnamed x1 -> x0, local copies, waits for them, and re-layouts: 1.26 us -> none
where the time goes in v2:
time: 28.2 us; the launch traced here: 28 us
  Pallas kernels  28 us (99%)
    pallas_call x1, Pallas kernels, body(): pl.pallas_call(lambda *refs: kernel(n_tp, *refs), out_shape=jax.ShapeDtyp...  26.7 us
    pallas_call x1, Pallas kernels, body(): pl.pallas_call(add_up, out_shape=jax.ShapeDtypeStruct((1, cols), bf16), n...  1.31 us

profile of v2, /device:TPU:1, one launch (start us, length us, event | category | flops | bytes accessed | tf_op | source)
XLA Modules:
  0.0 28.0 jit_solution(3963756474920255820)
XLA Ops:
  0.0 26.7 %paged_decode.1.parts_ref = f32[8,1,512]{2,1,0:T(1,128)} custom-call(s32[64]{0:T(128)} %refs_0_.1, s32[64]{0:T(128)} %refs_1_.1, bf16[1,1024]{1,0:T(2,128)(2,1)} %refs_2_.1, bf16[2,1,4096,128]{3,2,1,0:T(8,128)(2,1)} %refs_3_.1, bf16[2,1,4096,128]{3,2,1,0:T(8,128)(2,1)} %refs_4_.1, bf16[1024,4096]{1,0:T(8,128)(2,1)} %refs_5_.1), custom_call_target="tpu_custom_call" | custom-call | tf_op jit(solution)/shard_map/paged_decode/pallas_call | solution.py:226
  26.7 1.3 %add_up.1 = bf16[1,512]{1,0:T(2,128)(2,1)} custom-call(f32[8,1,512]{2,1,0:T(1,128)} %paged_decode.1.parts_ref), custom_call_target="tpu_custom_call" | custom-call | tf_op jit(solution)/shard_map/add_up/pallas_call | solution.py:256

commit v3 on v2

--- a/solution.py
+++ b/solution.py
@@ -31,7 +31,7 @@
     k_hbm,
     v_hbm,
     w_hbm,
-    out_hbm,
+    out_ref,
     req_ref,
     fill_ref,
     q_in,
@@ -43,6 +43,7 @@
     msg,
     got,
     part,
+    parts,
     local_sem,
     q_send,
     q_recv,
@@ -80,16 +81,9 @@
     req_copy = pltpu.make_async_copy(req_hbm, req_ref, local_sem.at[1])
     fill_copy = pltpu.make_async_copy(fill_hbm, fill_ref, local_sem.at[2])
     k_copy = pltpu.make_async_copy(k_hbm.at[:, 0], kbuf, local_sem.at[3])
-    v_copies = [
-        pltpu.make_async_copy(
-            v_hbm.at[b, 0],
-            vbuf.at[:, pl.ds(b * head_size, head_size)],
-            local_sem.at[4 + b],
-        )
-        for b in range(blocks)
-    ]
-    w_copy = pltpu.make_async_copy(w_hbm, wbuf, local_sem.at[4 + blocks])
-    for c in [q_copy, k_copy, req_copy, fill_copy] + v_copies + [w_copy]:
+    v_copy = pltpu.make_async_copy(v_hbm.at[:, 0], vbuf, local_sem.at[4])
+    w_copy = pltpu.make_async_copy(w_hbm, wbuf, local_sem.at[5])
+    for c in [q_copy, k_copy, req_copy, fill_copy, v_copy, w_copy]:
         c.start()
     q_copy.wait()
     for h in range(heads):
@@ -108,35 +102,29 @@
 
     k_copy.wait()
     for b in range(blocks):
-        kt[b * head_size : (b + 1) * head_size, :] = kbuf[b].T
+        kt[b] = kbuf[b].T
     req_copy.wait()
     fill_copy.wait()
-    for c in v_copies:
-        c.wait()
+    v_copy.wait()
     request = [req_ref[me * blocks + b] for b in range(blocks)]
     fill = [fill_ref[me * blocks + b] for b in range(blocks)]
 
     q_others = q_all.at[pl.ds(0, n_inst - 1)]
     pltpu.make_async_copy(q_others, q_others, q_recv).wait()
 
-    q = [q_all[pl.ds(r * STEPS, STEPS)].reshape(rows, head_size).astype(bf16) for r in request]
-    zero = jnp.zeros_like(q[0])
-    q = jnp.concatenate(
-        [jnp.concatenate([q[0], zero], axis=1), jnp.concatenate([zero, q[1]], axis=1)], axis=0
-    )
-    s = jnp.dot(q, kt[...], preferred_element_type=f32)
-    slot = lax.broadcasted_iota(jnp.int32, (rows, block_len), 1)
-    s = jnp.concatenate(
-        [jnp.where(slot < fill[b], s[b * rows : (b + 1) * rows], EMPTY) for b in range(blocks)],
-        axis=0,
-    )
-    top = (jnp.max(s, axis=1, keepdims=True) * scale).astype(bf16).astype(f32)
-    p = jnp.exp2(s * scale - top)
-    total = jnp.sum(p, axis=1, keepdims=True)
-    o = jnp.dot(p.astype(bf16), vbuf[...], preferred_element_type=f32)
-    tops = [top[:rows], top[rows:]]
-    totals = [total[:rows], total[rows:]]
-    outs = [o[:rows, :head_size], o[rows:, head_size:]]
+    scores = []
+    for b in range(blocks):
+        q = q_all[pl.ds(request[b] * STEPS, STEPS)].reshape(rows, head_size).astype(bf16)
+        scores.append(jnp.dot(q, kt[b], preferred_element_type=f32))
+    tops, totals, outs = [], [], []
+    for b in range(blocks):
+        slot = lax.broadcasted_iota(jnp.int32, (rows, block_len), 1)
+        s = jnp.where(slot < fill[b], scores[b], EMPTY)
+        top = (jnp.max(s, axis=1, keepdims=True) * scale).astype(bf16).astype(f32)
+        p = jnp.exp2(s * scale - top)
+        tops.append(top)
+        totals.append(jnp.sum(p, axis=1, keepdims=True))
+        outs.append(jnp.dot(p.astype(bf16), vbuf[b], preferred_element_type=f32))
 
     lane = lax.broadcasted_iota(jnp.int32, (rows, head_size), 1)
 
@@ -191,25 +179,19 @@
         if peer is not my_tp:
             pltpu.make_async_remote_copy(
                 src_ref=part.at[peer],
-                dst_ref=out_hbm.at[my_tp],
+                dst_ref=parts.at[my_tp],
                 send_sem=p_send,
                 recv_sem=p_recv,
                 device_id={"tp": peer},
                 device_id_type=MESH,
             ).start()
-    own = pltpu.make_async_copy(part.at[my_tp], out_hbm.at[my_tp], local_sem.at[0])
-    own.start()
+    parts[my_tp] = part[my_tp]
     pltpu.make_async_copy(q_others, q_others, q_send).wait()
     pltpu.make_async_copy(m_others, m_others, m_send).wait()
-    p_others = part.at[pl.ds(0, n_tp - 1)]
+    p_others = parts.at[pl.ds(0, n_tp - 1)]
     pltpu.make_async_copy(p_others, p_others, p_send).wait()
-    own.wait()
-    p_others = out_hbm.at[pl.ds(0, n_tp - 1)]
     pltpu.make_async_copy(p_others, p_others, p_recv).wait()
-
-
-def add_up(parts_ref, out_ref):
-    out_ref[...] = jnp.sum(parts_ref[...], axis=0).astype(out_ref.dtype)
+    out_ref[...] = jnp.sum(parts[...], axis=0).astype(out_ref.dtype)
 
 
 def solution(mesh):
@@ -223,24 +205,36 @@
         any_spec = pl.BlockSpec(memory_space=pl.ANY)
         dma = pltpu.SemaphoreType.DMA
         bf16, f32 = jnp.bfloat16, jnp.float32
-        parts = pl.pallas_call(
+        operands = [
+            pltpu.with_memory_space_constraint(a, pltpu.HBM)
+            for a in (
+                block_request,
+                block_fill,
+                queries,
+                cache_keys,
+                cache_values,
+                out_weight,
+            )
+        ]
+        return pl.pallas_call(
             lambda *refs: kernel(n_tp, *refs),
-            out_shape=jax.ShapeDtypeStruct((n_tp, 1, cols), f32),
+            out_shape=jax.ShapeDtypeStruct((1, cols), bf16),
             in_specs=[any_spec] * 6,
-            out_specs=any_spec,
+            out_specs=pl.BlockSpec(memory_space=pltpu.VMEM),
             scratch_shapes=[
                 pltpu.SMEM(block_request.shape, jnp.int32),
                 pltpu.SMEM(block_fill.shape, jnp.int32),
                 pltpu.VMEM(queries.shape, bf16),
                 pltpu.VMEM((blocks, block_len, head_size), bf16),
-                pltpu.VMEM((blocks * head_size, block_len), bf16),
-                pltpu.VMEM((block_len, blocks * head_size), bf16),
+                pltpu.VMEM((blocks, head_size, block_len), bf16),
+                pltpu.VMEM((blocks, block_len, head_size), bf16),
                 pltpu.VMEM((width, dout), bf16),
                 pltpu.VMEM((n_inst, heads, head_size), f32),
                 pltpu.VMEM((n_inst, 2 * heads, head_size), bf16),
                 pltpu.VMEM((n_inst, 2 * heads, head_size), bf16),
                 pltpu.VMEM((n_tp, 1, cols), f32),
-                dma((5 + blocks,)),
+                pltpu.VMEM((n_tp, 1, cols), f32),
+                dma((6,)),
                 dma,
                 dma,
                 dma,
@@ -249,15 +243,10 @@
                 dma,
             ],
             compiler_params=pltpu.CompilerParams(
-                collective_id=0, has_side_effects=True, vmem_limit_bytes=60 * 1024 * 1024
+                collective_id=0, has_side_effects=True, vmem_limit_bytes=40 * 1024 * 1024
             ),
             name="paged_decode",
-        )(block_request, block_fill, queries, cache_keys, cache_values, out_weight)
-        return pl.pallas_call(
-            add_up,
-            out_shape=jax.ShapeDtypeStruct((1, cols), bf16),
-            name="add_up",
-        )(parts)
+        )(*operands)
 
     in_specs = (
         P("inst", "tp"),

time: 28.2 us -> 26.5 us (0.940)
  Pallas kernels: 28 us -> 25.9 us
  local copies, waits for them, and re-layouts: 0 us -> 0.58 us
    pallas_call x1 -> x0, Pallas kernels: 1.31 us -> none  [body(): pl.pallas_call(add_up, out_shape=jax.ShapeDtypeStruct((1, cols), bf16), n...]
    pallas_call x1, Pallas kernels: 26.7 us -> 25.9 us  [body(): pl.pallas_call(lambda *refs: kernel(n_tp, *refs), out_shape=jax.ShapeDtyp...]
    unnamed x0 -> x1, local copies, waits for them, and re-layouts: none -> 0.58 us
where the time goes in v3:
time: 26.5 us; the launch traced here: 26.4 us
  Pallas kernels  25.9 us (98%)
  local copies, waits for them, and re-layouts  0.58 us (2%)
    pallas_call x1, Pallas kernels, body(): pl.pallas_call(lambda *refs: kernel(n_tp, *refs), out_shape=jax.ShapeDtyp...  25.9 us
    unnamed x1, local copies, waits for them, and re-layouts  0.58 us

profile of v3, /device:TPU:1, one launch (start us, length us, event | category | flops | bytes accessed | tf_op | source)
XLA Modules:
  0.0 26.4 jit_solution(3351310508762662211)
XLA Ops:
  0.0 25.9 %paged_decode.1 = bf16[1,512]{1,0:T(2,128)(2,1)S(1)} custom-call(s32[64]{0:T(128)} %refs_0_.1, s32[64]{0:T(128)} %refs_1_.1, bf16[1,1024]{1,0:T(2,128)(2,1)} %refs_2_.1, bf16[2,1,4096,128]{3,2,1,0:T(8,128)(2,1)} %refs_3_.1, bf16[2,1,4096,128]{3,2,1,0:T(8,128)(2,1)} %refs_4_.1, bf16[1024,4096]{1,0:T(8,128)(2,1)} %refs_5_.1), custom_call_target="tpu_custom_call" | custom-call | tf_op jit(solution)/shard_map/paged_decode/pallas_call | solution.py:219
  25.9 0.6 %copy.8 = bf16[1,512]{1,0:T(2,128)(2,1)} copy(bf16[1,512]{1,0:T(2,128)(2,1)S(1)} %paged_decode.1) | data formatting | bytes 2048

commit v4 on v3

--- a/solution.py
+++ b/solution.py
@@ -1,3 +1,4 @@
+import functools
 import math
 
 import jax
@@ -17,9 +18,9 @@
     return min(d, n - d)
 
 
-PLANE = sorted(
-    [(x, y, c) for x in range(SIDE) for y in range(SIDE) for c in range(2)][1:],
-    key=lambda d: -(ring(d[0], SIDE) + ring(d[1], SIDE) + 0.5 * d[2]),
+CHIPS = sorted(
+    [(x, y) for x in range(SIDE) for y in range(SIDE)][1:],
+    key=lambda d: -(ring(d[0], SIDE) + ring(d[1], SIDE)),
 )
 
 
@@ -63,10 +64,11 @@
     f32, bf16 = jnp.float32, jnp.bfloat16
 
     my_x, my_y, my_core = me // (2 * SIDE), (me // 2) % SIDE, me % 2
-    plane = [
-        (((my_x + x) % SIDE) * SIDE + (my_y + y) % SIDE) * 2 + (my_core + c) % 2
-        for x, y, c in PLANE
-    ]
+    plane = []
+    for x, y in CHIPS:
+        chip = ((my_x + x) % SIDE) * SIDE + (my_y + y) % SIDE
+        plane += [2 * chip, 2 * chip + 1]
+    plane.append(me + 1 - 2 * my_core)
     z_ring = [
         (my_tp + d) % n_tp for d in sorted(range(1, n_tp), key=lambda d: -ring(d, n_tp))
     ]
@@ -83,11 +85,13 @@
     k_copy = pltpu.make_async_copy(k_hbm.at[:, 0], kbuf, local_sem.at[3])
     v_copy = pltpu.make_async_copy(v_hbm.at[:, 0], vbuf, local_sem.at[4])
     w_copy = pltpu.make_async_copy(w_hbm, wbuf, local_sem.at[5])
-    for c in [q_copy, k_copy, req_copy, fill_copy, v_copy, w_copy]:
+    for c in [q_copy, k_copy, req_copy, fill_copy, v_copy]:
         c.start()
     q_copy.wait()
-    for h in range(heads):
-        q_all[me, h : h + 1, :] = q_in[:, h * head_size : (h + 1) * head_size].astype(f32)
+    own_q = q_in[...].astype(f32)
+    q_all[me] = jnp.concatenate(
+        [own_q[:, h * head_size : (h + 1) * head_size] for h in range(heads)], axis=0
+    ).astype(bf16)
     pl.semaphore_wait(barrier, len(plane) + len(z_ring))
 
     for peer in plane:
@@ -100,6 +104,8 @@
             device_id_type=MESH,
         ).start()
 
+    w_copy.start()
+
     k_copy.wait()
     for b in range(blocks):
         kt[b] = kbuf[b].T
@@ -114,7 +120,7 @@
 
     scores = []
     for b in range(blocks):
-        q = q_all[pl.ds(request[b] * STEPS, STEPS)].reshape(rows, head_size).astype(bf16)
+        q = q_all[pl.ds(request[b] * STEPS, STEPS)].reshape(rows, head_size)
         scores.append(jnp.dot(q, kt[b], preferred_element_type=f32))
     tops, totals, outs = [], [], []
     for b in range(blocks):
@@ -150,7 +156,7 @@
         msg[r * STEPS : (r + 1) * STEPS] = jnp.where(
             request[0] == r, first, jnp.where(request[1] == r, second, empty)
         )
-    for peer in plane:
+    def send_m(peer):
         pltpu.make_async_remote_copy(
             src_ref=msg.at[peer],
             dst_ref=got.at[me],
@@ -159,6 +165,10 @@
             device_id={"inst": peer},
             device_id_type=MESH,
         ).start()
+
+    pl.when(me != 1)(lambda: send_m(1))
+    for peer in plane:
+        pl.when(peer != 1)(functools.partial(send_m, peer))
     got[me] = msg[me]
     w_copy.wait()
     m_others = got.at[pl.ds(0, n_inst - 1)]
@@ -173,18 +183,24 @@
     att = jnp.sum(weight * o, axis=0) / jnp.sum(weight, axis=0)
     att = jnp.concatenate([att[h : h + 1] for h in range(heads)], axis=1).astype(bf16)
 
-    for peer in z_ring + [my_tp]:
+    def project(peer):
         cols = pl.ds(pl.multiple_of(peer * out_cols, out_cols), out_cols)
         part[peer] = jnp.dot(att, wbuf[:, cols], preferred_element_type=f32)
-        if peer is not my_tp:
-            pltpu.make_async_remote_copy(
-                src_ref=part.at[peer],
-                dst_ref=parts.at[my_tp],
-                send_sem=p_send,
-                recv_sem=p_recv,
-                device_id={"tp": peer},
-                device_id_type=MESH,
-            ).start()
+
+    def send_p(peer):
+        pltpu.make_async_remote_copy(
+            src_ref=part.at[peer],
+            dst_ref=parts.at[my_tp],
+            send_sem=p_send,
+            recv_sem=p_recv,
+            device_id={"tp": peer},
+            device_id_type=MESH,
+        ).start()
+
+    for peer in z_ring:
+        project(peer)
+        send_p(peer)
+    project(my_tp)
     parts[my_tp] = part[my_tp]
     pltpu.make_async_copy(q_others, q_others, q_send).wait()
     pltpu.make_async_copy(m_others, m_others, m_send).wait()
@@ -229,7 +245,7 @@
                 pltpu.VMEM((blocks, head_size, block_len), bf16),
                 pltpu.VMEM((blocks, block_len, head_size), bf16),
                 pltpu.VMEM((width, dout), bf16),
-                pltpu.VMEM((n_inst, heads, head_size), f32),
+                pltpu.VMEM((n_inst, heads, head_size), bf16),
                 pltpu.VMEM((n_inst, 2 * heads, head_size), bf16),
                 pltpu.VMEM((n_inst, 2 * heads, head_size), bf16),
                 pltpu.VMEM((n_tp, 1, cols), f32),

time: 26.5 us -> 26 us (0.981)
  Pallas kernels: 25.9 us -> 25.3 us
    pallas_call x1, Pallas kernels: 25.9 us -> 25.3 us  [body(): pl.pallas_call(lambda *refs: kernel(n_tp, *refs), out_shape=jax.ShapeDtyp...]
where the time goes in v4:
time: 26 us; the launch traced here: 25.9 us
  Pallas kernels  25.3 us (97%)
  local copies, waits for them, and re-layouts  0.58 us (2%)
    pallas_call x1, Pallas kernels, body(): pl.pallas_call(lambda *refs: kernel(n_tp, *refs), out_shape=jax.ShapeDtyp...  25.3 us
    unnamed x1, local copies, waits for them, and re-layouts  0.58 us

profile of v4, /device:TPU:1, one launch (start us, length us, event | category | flops | bytes accessed | tf_op | source)
XLA Modules:
  0.0 25.9 jit_solution(2249680497139589729)
XLA Ops:
  0.0 25.3 %paged_decode.1 = bf16[1,512]{1,0:T(2,128)(2,1)S(1)} custom-call(s32[64]{0:T(128)} %refs_0_.1, s32[64]{0:T(128)} %refs_1_.1, bf16[1,1024]{1,0:T(2,128)(2,1)} %refs_2_.1, bf16[2,1,4096,128]{3,2,1,0:T(8,128)(2,1)} %refs_3_.1, bf16[2,1,4096,128]{3,2,1,0:T(8,128)(2,1)} %refs_4_.1, bf16[1024,4096]{1,0:T(8,128)(2,1)} %refs_5_.1), custom_call_target="tpu_custom_call" | custom-call | tf_op jit(solution)/shard_map/paged_decode/pallas_call | solution.py:235
  25.3 0.6 %copy.8 = bf16[1,512]{1,0:T(2,128)(2,1)} copy(bf16[1,512]{1,0:T(2,128)(2,1)S(1)} %paged_decode.1) | data formatting | bytes 2048

commit v5 on v4

--- a/solution.py
+++ b/solution.py
@@ -1,4 +1,3 @@
-import functools
 import math
 
 import jax
@@ -46,6 +45,8 @@
     part,
     parts,
     local_sem,
+    pair_send,
+    pair_recv,
     q_send,
     q_recv,
     m_send,
@@ -64,20 +65,24 @@
     f32, bf16 = jnp.float32, jnp.bfloat16
 
     my_x, my_y, my_core = me // (2 * SIDE), (me // 2) % SIDE, me % 2
-    plane = []
-    for x, y in CHIPS:
-        chip = ((my_x + x) % SIDE) * SIDE + (my_y + y) % SIDE
-        plane += [2 * chip, 2 * chip + 1]
-    plane.append(me + 1 - 2 * my_core)
+    chips = [((my_x + x) % SIDE) * SIDE + (my_y + y) % SIDE for x, y in CHIPS]
+    sibling = me + 1 - 2 * my_core
+    plane = [2 * chip + core for chip in chips for core in range(2)] + [sibling]
     z_ring = [
         (my_tp + d) % n_tp for d in sorted(range(1, n_tp), key=lambda d: -ring(d, n_tp))
     ]
 
     barrier = pltpu.get_barrier_semaphore()
-    for peer in plane:
-        pl.semaphore_signal(barrier, inc=1, device_id={"inst": peer}, device_id_type=MESH)
+    my_lead = me + 1 - my_core
+    for chip in chips:
+        pl.semaphore_signal(
+            barrier, inc=1, device_id={"inst": 2 * chip + 1}, device_id_type=MESH
+        )
+    pl.semaphore_signal(barrier, inc=1, device_id={"inst": sibling}, device_id_type=MESH)
     for peer in z_ring:
-        pl.semaphore_signal(barrier, inc=1, device_id={"tp": peer}, device_id_type=MESH)
+        pl.semaphore_signal(
+            barrier, inc=1, device_id={"inst": my_lead, "tp": peer}, device_id_type=MESH
+        )
 
     q_copy = pltpu.make_async_copy(q_hbm, q_in, local_sem.at[0])
     req_copy = pltpu.make_async_copy(req_hbm, req_ref, local_sem.at[1])
@@ -92,17 +97,36 @@
     q_all[me] = jnp.concatenate(
         [own_q[:, h * head_size : (h + 1) * head_size] for h in range(heads)], axis=0
     ).astype(bf16)
-    pl.semaphore_wait(barrier, len(plane) + len(z_ring))
-
-    for peer in plane:
-        pltpu.make_async_remote_copy(
-            src_ref=q_all.at[me],
-            dst_ref=q_all.at[me],
-            send_sem=q_send,
-            recv_sem=q_recv,
-            device_id={"inst": peer},
-            device_id_type=MESH,
-        ).start()
+    pair = pltpu.make_async_remote_copy(
+        src_ref=q_all.at[me],
+        dst_ref=q_all.at[me],
+        send_sem=pair_send,
+        recv_sem=pair_recv,
+        device_id={"inst": sibling},
+        device_id_type=MESH,
+    )
+    q_others = q_all.at[pl.ds(0, n_inst - 2)]
+
+    @pl.when(my_core == 0)
+    def _():
+        pl.semaphore_wait(barrier, 1)
+        pair.start()
+
+    @pl.when(my_core == 1)
+    def _():
+        pl.semaphore_wait(barrier, 2 * len(chips) + 2 * len(z_ring) + 1)
+        pair.wait_recv()
+        rows_here = q_all.at[pl.ds(me - 1, 2)]
+        for peer in plane[:-1]:
+            pltpu.make_async_remote_copy(
+                src_ref=rows_here,
+                dst_ref=rows_here,
+                send_sem=q_send,
+                recv_sem=q_recv,
+                device_id={"inst": peer},
+                device_id_type=MESH,
+            ).start()
+        pair.start()
 
     w_copy.start()
 
@@ -115,14 +139,17 @@
     request = [req_ref[me * blocks + b] for b in range(blocks)]
     fill = [fill_ref[me * blocks + b] for b in range(blocks)]
 
-    q_others = q_all.at[pl.ds(0, n_inst - 1)]
+    @pl.when(my_core == 0)
+    def _():
+        pair.wait_recv()
+
     pltpu.make_async_copy(q_others, q_others, q_recv).wait()
 
     scores = []
     for b in range(blocks):
         q = q_all[pl.ds(request[b] * STEPS, STEPS)].reshape(rows, head_size)
         scores.append(jnp.dot(q, kt[b], preferred_element_type=f32))
-    tops, totals, outs = [], [], []
+    tops, totals, probs = [], [], []
     for b in range(blocks):
         slot = lax.broadcasted_iota(jnp.int32, (rows, block_len), 1)
         s = jnp.where(slot < fill[b], scores[b], EMPTY)
@@ -130,28 +157,37 @@
         p = jnp.exp2(s * scale - top)
         tops.append(top)
         totals.append(jnp.sum(p, axis=1, keepdims=True))
-        outs.append(jnp.dot(p.astype(bf16), vbuf[b], preferred_element_type=f32))
-
+        probs.append(p.astype(bf16))
+
+    same = request[0] == request[1]
+    top = jnp.maximum(tops[0], tops[1])
+    w0, w1 = [jnp.exp2(t - top) for t in tops]
+    total = w0 * totals[0] + w1 * totals[1]
+    w0, w1 = w0 / total, w1 / total
+    i0, i1 = 1.0 / totals[0], 1.0 / totals[1]
+    zero = jnp.zeros_like(i0)
+    weights = [
+        (jnp.where(same, w0, i0), jnp.where(same, w1, zero)),
+        (jnp.where(same, w0, zero), jnp.where(same, w1, i1)),
+    ]
+    half = head_size // 2
     lane = lax.broadcasted_iota(jnp.int32, (rows, head_size), 1)
-
-    def pack(top, total, o):
-        o = o * (1.0 / total)
-        high = total.astype(bf16).astype(f32)
-        stats = jnp.where(lane == 0, top, jnp.where(lane == 1, high, total - high))
-        o = o.reshape(STEPS, heads, head_size)
-        stats = stats.reshape(STEPS, heads, head_size)
-        return jnp.concatenate([o, stats], axis=1).astype(bf16)
-
-    both_top = jnp.maximum(tops[0], tops[1])
-    w0 = jnp.exp2(tops[0] - both_top)
-    w1 = jnp.exp2(tops[1] - both_top)
-    both = pack(both_top, w0 * totals[0] + w1 * totals[1], w0 * outs[0] + w1 * outs[1])
-    same = request[0] == request[1]
-    first = jnp.where(same, both, pack(tops[0], totals[0], outs[0]))
-    second = jnp.where(same, both, pack(tops[1], totals[1], outs[1]))
+    stats = []
+    for b in range(blocks):
+        m = jnp.where(same, top, tops[b])
+        n = jnp.where(same, total, totals[b])
+        stats.append(jnp.where(lane < half, m, n))
+    outs = [jnp.dot(probs[b], vbuf[b], preferred_element_type=f32) for b in range(blocks)]
+    shape = (STEPS, heads, head_size)
+    first, second = [
+        jnp.concatenate(
+            [(u * outs[0] + v * outs[1]).reshape(shape), stats[b].reshape(shape)], axis=1
+        ).astype(bf16)
+        for b, (u, v) in enumerate(weights)
+    ]
     row = lax.broadcasted_iota(jnp.int32, (STEPS, 2 * heads, head_size), 1)
     lanes = lax.broadcasted_iota(jnp.int32, (STEPS, 2 * heads, head_size), 2)
-    empty = jnp.where((row >= heads) & (lanes == 0), EMPTY, 0.0).astype(bf16)
+    empty = jnp.where((row >= heads) & (lanes < half), EMPTY, 0.0).astype(bf16)
     for r in range(requests):
         msg[r * STEPS : (r + 1) * STEPS] = jnp.where(
             request[0] == r, first, jnp.where(request[1] == r, second, empty)
@@ -166,21 +202,21 @@
             device_id_type=MESH,
         ).start()
 
-    pl.when(me != 1)(lambda: send_m(1))
-    for peer in plane:
-        pl.when(peer != 1)(functools.partial(send_m, peer))
+    send_m(jnp.where(me == 1, plane[0], 1))
+    for peer in plane[1:]:
+        send_m(jnp.where((peer == 1) & (me != 1), plane[0], peer))
     got[me] = msg[me]
     w_copy.wait()
     m_others = got.at[pl.ds(0, n_inst - 1)]
     pltpu.make_async_copy(m_others, m_others, m_recv).wait()
 
     tile = got[...].astype(f32)
-    o = tile[:, :heads]
-    top = tile[:, heads:, 0:1]
-    total = tile[:, heads:, 1:2] + tile[:, heads:, 2:3]
-    best = jnp.max(top, axis=0, keepdims=True)
-    weight = jnp.exp2(top - best) * total
-    att = jnp.sum(weight * o, axis=0) / jnp.sum(weight, axis=0)
+    o, stat = tile[:, :heads], tile[:, heads:]
+    other = pltpu.roll(stat, half, 2)
+    low = lax.broadcasted_iota(jnp.int32, stat.shape, 2) < half
+    top = jnp.where(low, stat, other)
+    weight = jnp.exp2(top - jnp.max(top, axis=0)) * jnp.where(low, other, stat)
+    att = jnp.sum(weight * o, axis=0) * (1.0 / jnp.sum(weight, axis=0))
     att = jnp.concatenate([att[h : h + 1] for h in range(heads)], axis=1).astype(bf16)
 
     def project(peer):
@@ -202,7 +238,13 @@
         send_p(peer)
     project(my_tp)
     parts[my_tp] = part[my_tp]
-    pltpu.make_async_copy(q_others, q_others, q_send).wait()
+    pair.wait_send()
+
+    @pl.when(my_core == 1)
+    def _():
+        for _ in range(2):
+            pltpu.make_async_copy(q_others, q_others, q_send).wait()
+
     pltpu.make_async_copy(m_others, m_others, m_send).wait()
     p_others = parts.at[pl.ds(0, n_tp - 1)]
     pltpu.make_async_copy(p_others, p_others, p_send).wait()
@@ -257,6 +299,8 @@
                 dma,
                 dma,
                 dma,
+                dma,
+                dma,
             ],
             compiler_params=pltpu.CompilerParams(
                 collective_id=0, has_side_effects=True, vmem_limit_bytes=40 * 1024 * 1024

time: 26 us -> 25.6 us (0.985)
  Pallas kernels: 25.3 us -> 24.9 us
    pallas_call x1, Pallas kernels: 25.3 us -> 24.9 us  [body(): pl.pallas_call(lambda *refs: kernel(n_tp, *refs), out_shape=jax.ShapeDtyp...]
where the time goes in v5:
time: 25.6 us; the launch traced here: 25.5 us
  Pallas kernels  24.9 us (97%)
  local copies, waits for them, and re-layouts  0.58 us (2%)
    pallas_call x1, Pallas kernels, body(): pl.pallas_call(lambda *refs: kernel(n_tp, *refs), out_shape=jax.ShapeDtyp...  24.9 us
    unnamed x1, local copies, waits for them, and re-layouts  0.58 us

profile of v5, /device:TPU:1, one launch (start us, length us, event | category | flops | bytes accessed | tf_op | source)
XLA Modules:
  0.0 25.5 jit_solution(5058540350088582166)
XLA Ops:
  0.0 24.9 %paged_decode.1 = bf16[1,512]{1,0:T(2,128)(2,1)S(1)} custom-call(s32[64]{0:T(128)} %refs_0_.1, s32[64]{0:T(128)} %refs_1_.1, bf16[1,1024]{1,0:T(2,128)(2,1)} %refs_2_.1, bf16[2,1,4096,128]{3,2,1,0:T(8,128)(2,1)} %refs_3_.1, bf16[2,1,4096,128]{3,2,1,0:T(8,128)(2,1)} %refs_4_.1, bf16[1024,4096]{1,0:T(8,128)(2,1)} %refs_5_.1), custom_call_target="tpu_custom_call" | custom-call | tf_op jit(solution)/shard_map/paged_decode/pallas_call | solution.py:277
  25.0 0.6 %copy.8 = bf16[1,512]{1,0:T(2,128)(2,1)} copy(bf16[1,512]{1,0:T(2,128)(2,1)S(1)} %paged_decode.1) | data formatting | bytes 2048

commit v6 on v5

--- a/solution.py
+++ b/solution.py
@@ -45,6 +45,7 @@
     part,
     parts,
     local_sem,
+    go,
     pair_send,
     pair_recv,
     q_send,
@@ -107,26 +108,34 @@
     )
     q_others = q_all.at[pl.ds(0, n_inst - 2)]
 
-    @pl.when(my_core == 0)
-    def _():
-        pl.semaphore_wait(barrier, 1)
-        pair.start()
-
-    @pl.when(my_core == 1)
-    def _():
-        pl.semaphore_wait(barrier, 2 * len(chips) + 2 * len(z_ring) + 1)
-        pair.wait_recv()
-        rows_here = q_all.at[pl.ds(me - 1, 2)]
-        for peer in plane[:-1]:
+    rows_here = q_all.at[pl.ds(my_lead - 1, 2)]
+
+    def send_q(core):
+        for chip in chips:
             pltpu.make_async_remote_copy(
                 src_ref=rows_here,
                 dst_ref=rows_here,
                 send_sem=q_send,
                 recv_sem=q_recv,
-                device_id={"inst": peer},
+                device_id={"inst": 2 * chip + core},
                 device_id_type=MESH,
             ).start()
+
+    @pl.when(my_core == 0)
+    def _():
+        pl.semaphore_wait(barrier, 1)
         pair.start()
+        pair.wait_recv()
+        pl.semaphore_wait(go, 1)
+        send_q(1)
+
+    @pl.when(my_core == 1)
+    def _():
+        pair.wait_recv()
+        pair.start()
+        pl.semaphore_wait(barrier, 2 * len(chips) + 2 * len(z_ring) + 1)
+        pl.semaphore_signal(go, inc=1, device_id={"inst": sibling}, device_id_type=MESH)
+        send_q(0)
 
     w_copy.start()
 
@@ -138,10 +147,6 @@
     v_copy.wait()
     request = [req_ref[me * blocks + b] for b in range(blocks)]
     fill = [fill_ref[me * blocks + b] for b in range(blocks)]
-
-    @pl.when(my_core == 0)
-    def _():
-        pair.wait_recv()
 
     pltpu.make_async_copy(q_others, q_others, q_recv).wait()
 
@@ -240,10 +245,7 @@
     parts[my_tp] = part[my_tp]
     pair.wait_send()
 
-    @pl.when(my_core == 1)
-    def _():
-        for _ in range(2):
-            pltpu.make_async_copy(q_others, q_others, q_send).wait()
+    pltpu.make_async_copy(q_others, q_others, q_send).wait()
 
     pltpu.make_async_copy(m_others, m_others, m_send).wait()
     p_others = parts.at[pl.ds(0, n_tp - 1)]
@@ -293,6 +295,7 @@
                 pltpu.VMEM((n_tp, 1, cols), f32),
                 pltpu.VMEM((n_tp, 1, cols), f32),
                 dma((6,)),
+                pltpu.SemaphoreType.REGULAR,
                 dma,
                 dma,
                 dma,

time: 25.6 us -> 25.4 us (level)
  no operation moved by 1% of the time
where the time goes in v6:
time: 25.4 us; the launch traced here: 25.3 us
  Pallas kernels  24.7 us (97%)
  local copies, waits for them, and re-layouts  0.58 us (2%)
    pallas_call x1, Pallas kernels, body(): pl.pallas_call(lambda *refs: kernel(n_tp, *refs), out_shape=jax.ShapeDtyp...  24.7 us
    unnamed x1, local copies, waits for them, and re-layouts  0.58 us

profile of v6, /device:TPU:1, one launch (start us, length us, event | category | flops | bytes accessed | tf_op | source)
XLA Modules:
  0.0 25.3 jit_solution(5788806485656670779)
XLA Ops:
  0.0 24.7 %paged_decode.1 = bf16[1,512]{1,0:T(2,128)(2,1)S(1)} custom-call(s32[64]{0:T(128)} %refs_0_.1, s32[64]{0:T(128)} %refs_1_.1, bf16[1,1024]{1,0:T(2,128)(2,1)} %refs_2_.1, bf16[2,1,4096,128]{3,2,1,0:T(8,128)(2,1)} %refs_3_.1, bf16[2,1,4096,128]{3,2,1,0:T(8,128)(2,1)} %refs_4_.1, bf16[1024,4096]{1,0:T(8,128)(2,1)} %refs_5_.1), custom_call_target="tpu_custom_call" | custom-call | tf_op jit(solution)/shard_map/paged_decode/pallas_call | solution.py:279
  24.7 0.6 %copy.8 = bf16[1,512]{1,0:T(2,128)(2,1)} copy(bf16[1,512]{1,0:T(2,128)(2,1)S(1)} %paged_decode.1) | data formatting | bytes 2048

commit v7 on v6

--- a/solution.py
+++ b/solution.py
@@ -39,6 +39,8 @@
     kt,
     vbuf,
     wbuf,
+    q_own,
+    q_other,
     q_all,
     msg,
     got,
@@ -58,7 +60,7 @@
     me = lax.axis_index("inst")
     my_tp = lax.axis_index("tp")
     blocks, block_len, head_size = kbuf.shape
-    n_inst, heads, _ = q_all.shape
+    n_inst, heads = msg.shape[0], q_own.shape[0]
     rows = STEPS * heads
     requests = n_inst // STEPS
     out_cols = part.shape[2]
@@ -95,20 +97,26 @@
         c.start()
     q_copy.wait()
     own_q = q_in[...].astype(f32)
-    q_all[me] = jnp.concatenate(
+    q_own[...] = jnp.concatenate(
         [own_q[:, h * head_size : (h + 1) * head_size] for h in range(heads)], axis=0
-    ).astype(bf16)
+    )
+
     pair = pltpu.make_async_remote_copy(
-        src_ref=q_all.at[me],
-        dst_ref=q_all.at[me],
+        src_ref=q_own,
+        dst_ref=q_other,
         send_sem=pair_send,
         recv_sem=pair_recv,
         device_id={"inst": sibling},
         device_id_type=MESH,
     )
-    q_others = q_all.at[pl.ds(0, n_inst - 2)]
-
-    rows_here = q_all.at[pl.ds(my_lead - 1, 2)]
+    q_others = q_all.at[pl.ds(0, len(chips))]
+
+    rows_here = q_all.at[me // 2]
+
+    def join():
+        own, other = q_own[...], q_other[...]
+        low, high = jnp.where(my_core == 0, own, other), jnp.where(my_core == 0, other, own)
+        q_all[me // 2] = jnp.concatenate([low, high], axis=0).astype(bf16)
 
     def send_q(core):
         for chip in chips:
@@ -126,6 +134,7 @@
         pl.semaphore_wait(barrier, 1)
         pair.start()
         pair.wait_recv()
+        join()
         pl.semaphore_wait(go, 1)
         send_q(1)
 
@@ -133,6 +142,7 @@
     def _():
         pair.wait_recv()
         pair.start()
+        join()
         pl.semaphore_wait(barrier, 2 * len(chips) + 2 * len(z_ring) + 1)
         pl.semaphore_signal(go, inc=1, device_id={"inst": sibling}, device_id_type=MESH)
         send_q(0)
@@ -152,7 +162,7 @@
 
     scores = []
     for b in range(blocks):
-        q = q_all[pl.ds(request[b] * STEPS, STEPS)].reshape(rows, head_size)
+        q = q_all[pl.ds(request[b] * (STEPS // 2), STEPS // 2)].reshape(rows, head_size)
         scores.append(jnp.dot(q, kt[b], preferred_element_type=f32))
     tops, totals, probs = [], [], []
     for b in range(blocks):
@@ -289,7 +299,9 @@
                 pltpu.VMEM((blocks, head_size, block_len), bf16),
                 pltpu.VMEM((blocks, block_len, head_size), bf16),
                 pltpu.VMEM((width, dout), bf16),
-                pltpu.VMEM((n_inst, heads, head_size), bf16),
+                pltpu.VMEM((heads, head_size), f32),
+                pltpu.VMEM((heads, head_size), f32),
+                pltpu.VMEM((n_inst // 2, 2 * heads, head_size), bf16),
                 pltpu.VMEM((n_inst, 2 * heads, head_size), bf16),
                 pltpu.VMEM((n_inst, 2 * heads, head_size), bf16),
                 pltpu.VMEM((n_tp, 1, cols), f32),

time: 25.4 us -> 25.4 us (level)
  no operation moved by 1% of the time
where the time goes in v7:
time: 25.4 us; the launch traced here: 25.3 us
  Pallas kernels  24.7 us (97%)
  local copies, waits for them, and re-layouts  0.58 us (2%)
    pallas_call x1, Pallas kernels, body(): pl.pallas_call(lambda *refs: kernel(n_tp, *refs), out_shape=jax.ShapeDtyp...  24.7 us
    unnamed x1, local copies, waits for them, and re-layouts  0.58 us

profile of v7, /device:TPU:1, one launch (start us, length us, event | category | flops | bytes accessed | tf_op | source)
XLA Modules:
  0.0 25.3 jit_solution(17630879568379162628)
XLA Ops:
  0.0 24.7 %paged_decode.1 = bf16[1,512]{1,0:T(2,128)(2,1)S(1)} custom-call(s32[64]{0:T(128)} %refs_0_.1, s32[64]{0:T(128)} %refs_1_.1, bf16[1,1024]{1,0:T(2,128)(2,1)} %refs_2_.1, bf16[2,1,4096,128]{3,2,1,0:T(8,128)(2,1)} %refs_3_.1, bf16[2,1,4096,128]{3,2,1,0:T(8,128)(2,1)} %refs_4_.1, bf16[1024,4096]{1,0:T(8,128)(2,1)} %refs_5_.1), custom_call_target="tpu_custom_call" | custom-call | tf_op jit(solution)/shard_map/paged_decode/pallas_call | solution.py:289
  24.7 0.6 %copy.8 = bf16[1,512]{1,0:T(2,128)(2,1)} copy(bf16[1,512]{1,0:T(2,128)(2,1)S(1)} %paged_decode.1) | data formatting | bytes 2048

commit v8 on v7

--- a/solution.py
+++ b/solution.py
@@ -1,3 +1,4 @@
+import functools
 import math
 
 import jax
@@ -52,6 +53,7 @@
     pair_recv,
     q_send,
     q_recv,
+    f_send,
     m_send,
     m_recv,
     p_send,
@@ -203,10 +205,6 @@
     row = lax.broadcasted_iota(jnp.int32, (STEPS, 2 * heads, head_size), 1)
     lanes = lax.broadcasted_iota(jnp.int32, (STEPS, 2 * heads, head_size), 2)
     empty = jnp.where((row >= heads) & (lanes < half), EMPTY, 0.0).astype(bf16)
-    for r in range(requests):
-        msg[r * STEPS : (r + 1) * STEPS] = jnp.where(
-            request[0] == r, first, jnp.where(request[1] == r, second, empty)
-        )
     def send_m(peer):
         pltpu.make_async_remote_copy(
             src_ref=msg.at[peer],
@@ -217,9 +215,34 @@
             device_id_type=MESH,
         ).start()
 
-    send_m(jnp.where(me == 1, plane[0], 1))
-    for peer in plane[1:]:
-        send_m(jnp.where((peer == 1) & (me != 1), plane[0], peer))
+    def fill_m(r, begin, end):
+        msg[r * STEPS + begin : r * STEPS + end] = jnp.where(
+            request[0] == r,
+            first[begin:end],
+            jnp.where(request[1] == r, second[begin:end], empty[begin:end]),
+        )
+
+    fill_m(0, 1, 2)
+    first_m = pltpu.make_async_remote_copy(
+        src_ref=msg.at[1],
+        dst_ref=got.at[me],
+        send_sem=f_send,
+        recv_sem=m_recv,
+        device_id={"inst": 1},
+        device_id_type=MESH,
+    )
+    pl.when(me != 1)(first_m.start)
+    fill_m(0, 0, 1)
+    fill_m(0, 2, STEPS)
+    for r in range(1, requests):
+        fill_m(r, 0, STEPS)
+    for chip in chips:
+        send_m(2 * chip)
+    pl.when(my_core == 1)(lambda: send_m(sibling))
+    pl.when(me != 1)(first_m.wait_send)
+    for chip in chips:
+        pl.when(chip != 0)(functools.partial(send_m, 2 * chip + 1))
+    pl.when((my_core == 0) & (me != 0))(lambda: send_m(sibling))
     got[me] = msg[me]
     w_copy.wait()
     m_others = got.at[pl.ds(0, n_inst - 1)]
@@ -257,7 +280,13 @@
 
     pltpu.make_async_copy(q_others, q_others, q_send).wait()
 
-    pltpu.make_async_copy(m_others, m_others, m_send).wait()
+    m_sent = msg.at[pl.ds(0, n_inst - 2)]
+    pltpu.make_async_copy(m_sent, m_sent, m_send).wait()
+
+    @pl.when(me == 1)
+    def _():
+        pltpu.make_async_copy(msg.at[0], msg.at[0], m_send).wait()
+
     p_others = parts.at[pl.ds(0, n_tp - 1)]
     pltpu.make_async_copy(p_others, p_others, p_send).wait()
     pltpu.make_async_copy(p_others, p_others, p_recv).wait()
@@ -316,6 +345,7 @@
                 dma,
                 dma,
                 dma,
+                dma,
             ],
             compiler_params=pltpu.CompilerParams(
                 collective_id=0, has_side_effects=True, vmem_limit_bytes=40 * 1024 * 1024

time: 25.4 us -> 25.4 us (level)
  no operation moved by 1% of the time
where the time goes in v8:
time: 25.4 us; the launch traced here: 25.3 us
  Pallas kernels  24.7 us (97%)
  local copies, waits for them, and re-layouts  0.58 us (2%)
    pallas_call x1, Pallas kernels, body(): pl.pallas_call(lambda *refs: kernel(n_tp, *refs), out_shape=jax.ShapeDtyp...  24.7 us
    unnamed x1, local copies, waits for them, and re-layouts  0.58 us

profile of v8, /device:TPU:1, one launch (start us, length us, event | category | flops | bytes accessed | tf_op | source)
XLA Modules:
  0.0 25.3 jit_solution(13848750835785412436)
XLA Ops:
  0.0 24.7 %paged_decode.1 = bf16[1,512]{1,0:T(2,128)(2,1)S(1)} custom-call(s32[64]{0:T(128)} %refs_0_.1, s32[64]{0:T(128)} %refs_1_.1, bf16[1,1024]{1,0:T(2,128)(2,1)} %refs_2_.1, bf16[2,1,4096,128]{3,2,1,0:T(8,128)(2,1)} %refs_3_.1, bf16[2,1,4096,128]{3,2,1,0:T(8,128)(2,1)} %refs_4_.1, bf16[1024,4096]{1,0:T(8,128)(2,1)} %refs_5_.1), custom_call_target="tpu_custom_call" | custom-call | tf_op jit(solution)/shard_map/paged_decode/pallas_call | solution.py:318
  24.7 0.6 %copy.8 = bf16[1,512]{1,0:T(2,128)(2,1)} copy(bf16[1,512]{1,0:T(2,128)(2,1)S(1)} %paged_decode.1) | data formatting | bytes 2048
